TPU v7x, 256 devices: a whole 4x4x8 slice. The times are simulated.
256 devices in a mesh: blk: 32 (over x_hi, z, core), grp: 8 (over y, x_lo).
Axes of the slice: x: 4 (x_hi: 2, x_lo: 2; x = x_hi * 2 + x_lo), y: 4, z: 8, core: 2. Of those that a mesh axis runs over, the one named last changes fastest.
Arguments:
- embedding: bfloat16 [262144, 512], P(('blk', 'grp')), may hold values from -2 to 2
- direction: float32 [262144, 32], P(('blk', 'grp'))
- residual: float32 [262144, 32], P(('blk', 'grp'))
- solution: float32 [262144, 32], P(('blk', 'grp')), may hold values from -6 to 6
- prior: float32 [262144, 32], P(('blk', 'grp')), may hold values from -6 to 6
- plan: int32 [255], replicated, may hold values from 1 to 255, as said below
- round_index: int32 [1], replicated, may hold values from 0 to 252
Outputs:
- new_solution: float32 [262144, 32], P(('blk', 'grp'))
- new_residual: float32 [262144, 32], P(('blk', 'grp'))
- new_direction: float32 [262144, 32], P(('blk', 'grp'))
Inputs may be any that keep to these rules, and one draw needn't show every extreme that they name: `plan`: every value 1 to 255 appears exactly once.
All inputs are finite; a program needn't handle non-finite values.
Results may differ from a plain program's by a relative error of at most 0.0049.
Values may be sent and summed in bfloat16 or wider, within the bound.
A program may use at most 64 MiB of HBM per device.

v0:
```python
import functools
import math

import jax
import jax.numpy as jnp
from jax import lax
from jax.experimental import pallas as pl
from jax.experimental.pallas import tpu as pltpu
from jax.sharding import PartitionSpec as P


ROUNDS = 3
GAMMA = 2.0
ROWS = 1024
DIM = 512
PROBES = 32
DEEP = 8
AXES = ("blk", "grp")
MESH = pl.DeviceIdType.MESH
VMEM = pl.BlockSpec(memory_space=pltpu.VMEM)
SMEM = pl.BlockSpec(memory_space=pltpu.SMEM)
ANY = pl.BlockSpec(memory_space=pl.ANY)
F32 = jnp.float32
BF16 = jnp.bfloat16
TALL = DIM + PROBES
PART = 352
STARTS = (0, 336, 672)
PIECE = PART // 2
CUTS = (0, 256, 640, 1024)
SCALE = -GAMMA * math.log2(math.e)
LOSS = 1e-2


def params(collective_id=None):
    return pltpu.CompilerParams(
        collective_id=collective_id,
        has_side_effects=collective_id is not None,
        vmem_limit_bytes=40 * 2**20,
    )


def prepare_kernel(x_ref, d_ref, out_ref, p0_ref, p1_ref, p2_ref):
    out_ref[:DIM] = x_ref[...].T
    out_ref[DIM:] = d_ref[...].astype(BF16)
    for ref, start in zip((p0_ref, p1_ref, p2_ref), STARTS):
        ref[...] = x_ref[start : start + PART]


def prepare(embedding, dir_t):
    part = jax.ShapeDtypeStruct((PART, DIM), BF16)
    return pl.pallas_call(
        prepare_kernel,
        out_shape=(jax.ShapeDtypeStruct((TALL, ROWS), BF16), part, part, part),
        in_specs=[VMEM] * 2,
        out_specs=(VMEM,) * 4,
        compiler_params=params(),
        name="prepare",
    )(embedding, dir_t)


def move_kernel(
    rest, part_ref, block_ref, ring_ref, b_ref,
    own_sem, b_send, b_recv, right_send, right_recv, left_send, left_recv,
):
    blk, grp = lax.axis_index("blk"), lax.axis_index("grp")
    z = lax.rem(lax.div(blk, 2), DEEP)
    base = blk - 2 * z
    right = (base + 2 * lax.rem(z + 1, DEEP), grp)
    left = (base + 2 * lax.rem(z + DEEP - 1, DEEP), grp)
    other = (blk ^ ((rest >> 4) << 4 | (rest >> 3) & 1), grp ^ (rest & 7))
    barrier = pltpu.get_barrier_semaphore()
    greeted = [right, left] + ([other] if rest else [])
    for device in greeted:
        pl.semaphore_signal(barrier, inc=1, device_id=device, device_id_type=MESH)
    own = pltpu.make_async_copy(part_ref, ring_ref.at[0], own_sem)
    own.start()
    pl.semaphore_wait(barrier, len(greeted))

    def hop(to, step, piece, send, recvs, sign):
        rows = pl.ds(piece * PIECE, PIECE)
        source = lax.rem(DEEP + sign * (step - 1), DEEP)
        target = lax.rem(DEEP + sign * step, DEEP)
        return pltpu.make_async_remote_copy(
            src_ref=ring_ref.at[source, rows],
            dst_ref=ring_ref.at[target, rows],
            send_sem=send,
            recv_sem=recvs.at[step - 1, piece],
            device_id=to,
            device_id_type=MESH,
        )

    def rightward(step, piece, send=right_send.at[0]):
        return hop(right, step, piece, send, right_recv, 1)

    def leftward(step, piece, send=left_send.at[0]):
        return hop(left, step, piece, send, left_recv, -1)

    def begin(piece, carry):
        rightward(1, piece).start()
        leftward(1, piece).start()
        return carry

    def pass_on(index, carry):
        step, piece = lax.div(index, 2), lax.rem(index, 2)
        rightward(step - 1, piece).wait_recv()
        rightward(step, piece).start()
        leftward(step - 1, piece).wait_recv()
        leftward(step, piece).start()
        return carry

    own.wait()
    lax.fori_loop(0, 2, begin, 0)
    if rest:
        direct = pltpu.make_async_remote_copy(
            src_ref=block_ref,
            dst_ref=b_ref,
            send_sem=b_send,
            recv_sem=b_recv,
            device_id=other,
            device_id_type=MESH,
        )
    else:
        direct = pltpu.make_async_copy(block_ref, b_ref, b_send)
    direct.start()
    lax.fori_loop(4, 8, pass_on, 0)
    rightward(3, 0).wait_recv()
    last_right = rightward(4, 0, right_send.at[1])
    last_right.start()
    leftward(3, 1).wait_recv()
    last_left = leftward(4, 1, left_send.at[1])
    last_left.start()
    rightward(3, 1).wait_recv()
    leftward(3, 0).wait_recv()
    for send in (right_send, left_send):
        whole = ring_ref.at[pl.ds(0, 3)]
        pltpu.make_async_remote_copy(
            src_ref=whole,
            dst_ref=whole,
            send_sem=send.at[0],
            recv_sem=right_recv.at[0, 0],
            device_id=right,
            device_id_type=MESH,
        ).wait_send()
    last_right.wait()
    last_left.wait()
    direct.wait()


def move(rest, part, block):
    one = pltpu.SemaphoreType.DMA
    sends, recvs = one((2,)), one((4, 2))
    return pl.pallas_call(
        functools.partial(move_kernel, rest),
        out_shape=(
            jax.ShapeDtypeStruct((DEEP, PART, DIM), BF16),
            jax.ShapeDtypeStruct((TALL, ROWS), BF16),
        ),
        in_specs=[ANY] * 2,
        out_specs=(ANY, ANY),
        scratch_shapes=[one, one, one, sends, recvs, sends, recvs],
        compiler_params=params(2 + rest),
        name=f"move_{rest}",
    )(part, block)


def move_by(rest, part, block):
    return lax.switch(rest, [functools.partial(move, k) for k in range(32)], part, block)


def tree(ref):
    v = ref[...]
    while v.shape[0] > 1:
        half = v.shape[0] // 2
        v = v[:half] + v[half:]
    return v[0]


def exchange(slots, send_sem, recv_sem, place):
    count = slots.shape[0]

    def send(k, carry):
        pltpu.make_async_remote_copy(
            src_ref=slots.at[0],
            dst_ref=slots.at[k],
            send_sem=send_sem,
            recv_sem=recv_sem,
            device_id=place(k),
            device_id_type=MESH,
        ).start()
        return carry

    lax.fori_loop(1, count, send, 0)
    whole = pltpu.make_async_remote_copy(
        src_ref=slots.at[pl.ds(1, count - 1)],
        dst_ref=slots.at[pl.ds(1, count - 1)],
        send_sem=send_sem,
        recv_sem=recv_sem,
        device_id=place(1),
        device_id_type=MESH,
    )
    whole.wait_recv()
    return whole


def finish_kernel(
    depth_ref, d_ref, r_ref, p_ref, g0_ref, g1_ref, g2_ref, b0_ref, b1_ref, b2_ref,
    image_ref, alpha_ref, beta_ref, bad_ref,
    g0, g1, g2, blocks, right_sq, terms, sent, back, near, far,
    part_sem, block_sem, back_send, back_recv, near_send, near_recv, far_send, far_recv,
):
    blk, grp = lax.axis_index("blk"), lax.axis_index("grp")
    z = lax.rem(lax.div(blk, 2), DEEP)

    def near_place(k):
        return (blk ^ ((k >> 3) << 4), grp ^ (k & 7))

    def far_place(k):
        return (blk ^ k, grp)

    barrier = pltpu.get_barrier_semaphore()

    def greet(k, carry):
        pl.semaphore_signal(barrier, inc=1, device_id=near_place(k), device_id_type=MESH)
        pl.semaphore_signal(barrier, inc=1, device_id=far_place(k), device_id_type=MESH)
        return carry

    lax.fori_loop(1, 16, greet, 0)

    def load_block(s):
        return pltpu.make_async_copy((b0_ref, b1_ref, b2_ref)[s], blocks.at[s], block_sem.at[s])

    def load_part(part):
        refs = ((g0_ref, g0), (g1_ref, g1), (g2_ref, g2))
        return pltpu.make_async_copy(*refs[part], part_sem.at[part])

    load_block(0).start()
    load_part(0).start()
    for s in range(1, ROUNDS):
        load_block(s).start()
    for part in range(1, ROUNDS):
        load_part(part).start()
    depths = [depth_ref[s] for s in range(ROUNDS)]
    pieces = []
    for part, gathered in enumerate((g0, g1, g2)):
        load_part(part).wait()

        def one_term(s, carry, part=part, gathered=gathered):
            if part == 0:
                pltpu.make_async_copy(b0_ref, blocks.at[s], block_sem.at[s]).wait()
                wide = blocks[s, :DIM].astype(F32)
                right_sq[s] = SCALE * jnp.sum(wide * wide, axis=0, keepdims=True)
            slot = (z - (z ^ depth_ref[s])) & (DEEP - 1)
            a = gathered[slot]
            wide = a.astype(F32)
            left_sq = SCALE * jnp.sum(wide * wide, axis=1, keepdims=True) + 1.0
            cross = jnp.dot(a, blocks[s, :DIM], preferred_element_type=F32)
            kern = jnp.exp2((left_sq + right_sq[s]) + (-2.0 * SCALE) * cross).astype(BF16)
            terms[s, :, STARTS[part] : STARTS[part] + PART] = lax.dot_general(
                blocks[s, DIM:], kern, (((1,), (1,)), ((), ())), preferred_element_type=F32
            )
            return carry

        lax.fori_loop(0, ROUNDS, one_term, 0)
        columns = slice(CUTS[part], CUTS[part + 1])
        lanes = pl.ds(CUTS[part], CUTS[part + 1] - CUTS[part])
        if part == 0:
            pl.semaphore_wait(barrier, 30)

        def give_back(k, carry, part=part, columns=columns, lanes=lanes):
            meant = sum(
                jnp.where(depths[s] == k, terms[s, :, columns], 0.0) for s in range(ROUNDS)
            )
            sent[k, :, columns] = meant.astype(BF16)
            pltpu.make_async_remote_copy(
                src_ref=sent.at[k, :, lanes],
                dst_ref=back.at[k, :, lanes],
                send_sem=back_send.at[part],
                recv_sem=back_recv.at[part],
                device_id=far_place(2 * k),
                device_id_type=MESH,
            ).start()
            return carry

        lax.fori_loop(1, DEEP, give_back, 0)
        pieces.append(
            pltpu.make_async_remote_copy(
                src_ref=sent.at[pl.ds(1, DEEP - 1), :, lanes],
                dst_ref=back.at[pl.ds(1, DEEP - 1), :, lanes],
                send_sem=back_send.at[part],
                recv_sem=back_recv.at[part],
                device_id=far_place(2),
                device_id_type=MESH,
            )
        )
    columns = [0.0] * 4
    for part, piece in enumerate(pieces):
        piece.wait_recv()
        cut = slice(CUTS[part], CUTS[part + 1])
        d, r = d_ref[:, cut], r_ref[:, cut]
        image = p_ref[:, cut] + d
        for s in range(ROUNDS):
            image = image + jnp.where(depths[s] == 0, terms[s, :, cut], 0.0)
        for k in range(1, DEEP):
            image = image + back[k, :, cut].astype(F32)
        image_ref[:, cut] = image
        for q, (a, b) in enumerate(((r, r), (d, image), (r, image), (image, image))):
            columns[q] = columns[q] + jnp.sum(a * b, axis=1, keepdims=True)
    lane = lax.broadcasted_iota(jnp.int32, (8, 128), 1)
    packed = jnp.zeros((8, 128), F32)
    for q, column in enumerate(columns):
        for g in range(4):
            packed = jnp.where(lane == q * 4 + g, column[g * 8 : g * 8 + 8], packed)
    near[0] = packed
    first = exchange(near, near_send, near_recv, near_place)
    far[0] = tree(near)
    second = exchange(far, far_send, far_recv, far_place)
    total = tree(far)
    norm, curv, cross, square = (
        jnp.concatenate([total[:, q * 4 + g : q * 4 + g + 1] for g in range(4)], axis=0)
        for q in range(4)
    )
    alpha = norm / curv
    alpha_ref[...] = alpha
    twice, quad = 2.0 * alpha * cross, alpha * alpha * square
    following = norm - twice + quad
    good = following >= LOSS * (norm + jnp.abs(twice) + quad)
    good = jnp.logical_and(good, following < 3e38)
    beta_ref[...] = following / norm
    bad_ref[0, 0] = jnp.max(jnp.where(good, 0.0, 1.0))
    bad_ref[0, 1] = 0.0
    for piece in pieces:
        piece.wait_send()
    first.wait_send()
    second.wait_send()


def finish(depths, dir_t, res_t, prior_t, parts, blocks):
    column = jax.ShapeDtypeStruct((PROBES, 1), F32)
    dma = pltpu.SemaphoreType.DMA
    return pl.pallas_call(
        finish_kernel,
        out_shape=(
            jax.ShapeDtypeStruct((PROBES, ROWS), F32),
            column,
            column,
            jax.ShapeDtypeStruct((1, 2), F32),
        ),
        in_specs=[SMEM] + [VMEM] * 3 + [ANY] * 6,
        out_specs=(VMEM, VMEM, VMEM, SMEM),
        scratch_shapes=[pltpu.VMEM((DEEP, PART, DIM), BF16)] * 3
        + [pltpu.VMEM((ROUNDS, TALL, ROWS), BF16), pltpu.VMEM((ROUNDS, 1, ROWS), F32)]
        + [pltpu.VMEM((ROUNDS, PROBES, ROWS), F32)]
        + [pltpu.VMEM((DEEP, PROBES, ROWS), BF16)] * 2
        + [pltpu.VMEM((16, 8, 128), F32)] * 2
        + [dma((3,))] * 4 + [dma] * 4,
        compiler_params=params(1),
        name="finish",
    )(depths, dir_t, res_t, prior_t, *parts, *blocks)


def result_kernel(d_ref, r_ref, s_ref, image_ref, alpha_ref, beta_ref, ns_ref, nr_ref, nd_ref):
    d, alpha = d_ref[...], alpha_ref[...]
    ns_ref[...] = s_ref[...] + alpha * d
    new_residual = r_ref[...] - alpha * image_ref[...]
    nr_ref[...] = new_residual
    nd_ref[...] = new_residual + beta_ref[...] * d


def result(*operands):
    shape = jax.ShapeDtypeStruct((PROBES, ROWS), F32)
    return pl.pallas_call(
        result_kernel,
        out_shape=(shape,) * 3,
        in_specs=[VMEM] * 6,
        out_specs=(VMEM,) * 3,
        compiler_params=params(),
        name="result",
    )(*operands)


def local(embedding, direction, residual, solution, prior, plan, round_index):
    dir_t, res_t = direction.T, residual.T
    masks = lax.dynamic_slice(plan, (round_index[0],), (ROUNDS,))
    depths = jnp.bitwise_and(masks >> 4, DEEP - 1)
    rests = jnp.bitwise_or((masks >> 7) << 4, jnp.bitwise_and(masks, 15))
    block, *own = prepare(embedding, dir_t)
    parts, blocks = [], []
    for step in range(ROUNDS):
        part, arrived = move_by(rests[step], own[step], block)
        parts.append(part)
        blocks.append(arrived)
    image, alpha, beta, bad = finish(depths, dir_t, res_t, prior.T, parts, blocks)

    def again():
        new_res = res_t - alpha * image
        norm = lax.psum(jnp.sum(res_t * res_t, axis=1, keepdims=True), AXES)
        return lax.psum(jnp.sum(new_res * new_res, axis=1, keepdims=True), AXES) / norm

    beta = lax.cond(bad[0, 0] > 0, again, lambda: beta)
    results = result(dir_t, res_t, solution.T, image, alpha, beta)
    return tuple(out.T for out in results)


def solution(mesh):
    rows = P(AXES, None)
    return jax.shard_map(
        local,
        mesh=mesh,
        in_specs=(rows,) * 5 + (P(), P()),
        out_specs=(rows,) * 3,
        check_vma=False,
    )
```

profile of v0, /device:TPU:1, one launch (start us, length us, event | category | flops | bytes accessed | tf_op | source)
XLA Modules:
  0.0 145.5 jit_solution(2854084988397829562)
XLA Ops:
  1.3 0.8 and_or_fusion
  2.0 0.6 fusion
  4.6 0.0 copy-start
  4.6 0.9 copy-done
  5.5 0.0 copy-start.2
  5.5 1.2 copy-done.2
  6.7 0.4 prepare.1
  7.1 38.9 %conditional.6 = ((bf16[8,352,512]{2,1,0:T(8,128)(2,1)}, bf16[544,1024]{1,0:T(8,128)(2,1)S(1)})) conditional(s32[]{:T(128)} %bitcast.10, (bf16[352,512]{1,0:T(8,128)(2,1)S(1)}, bf16[544,1024]{1,0:T(8,128)(2,1)S(1)}) %tuple.304, (bf16[352,512]{1,0:T(8,128)(2,1)S(1)}, bf16[544,1024]{1,0:T(8,128)(2,1)S(1)}) %tuple.304, ...), branch_computations={%region_64.0_spmd, %region_65.0_spmd, %region_66.0_spmd, %region_6... | conditional | bytes 8 | solution.py:167
  7.1 38.8 %move_12.5 = (bf16[8,352,512]{2,1,0:T(8,128)(2,1)}, bf16[544,1024]{1,0:T(8,128)(2,1)S(1)}) custom-call(bf16[352,512]{1,0:T(8,128)(2,1)S(1)} %get-tuple-element.546.part_ref, bf16[544,1024]{1,0:T(8,128)(2,1)S(1)} %get-tuple-element.547.block_ref), custom_call_target="tpu_custom_call" | custom-call | tf_op jit(solution)/shard_map/cond/branch_12_fun/move_12/pallas_call | solution.py:152
  46.0 36.9 %conditional.5 = ((bf16[8,352,512]{2,1,0:T(8,128)(2,1)}, bf16[544,1024]{1,0:T(8,128)(2,1)})) conditional(s32[]{:T(128)} %bitcast.9, (bf16[352,512]{1,0:T(8,128)(2,1)S(1)}, bf16[544,1024]{1,0:T(8,128)(2,1)S(1)}) %tuple.303, (bf16[352,512]{1,0:T(8,128)(2,1)S(1)}, bf16[544,1024]{1,0:T(8,128)(2,1)S(1)}) %tuple.303, ...), branch_computations={%region_32.0_spmd, %region_33.0_spmd, %region_34.0_spmd, %region_3... | conditional | bytes 8 | solution.py:167
  46.3 36.6 %move_27.4 = (bf16[8,352,512]{2,1,0:T(8,128)(2,1)}, bf16[544,1024]{1,0:T(8,128)(2,1)}) custom-call(bf16[352,512]{1,0:T(8,128)(2,1)S(1)} %get-tuple-element.512.part_ref, bf16[544,1024]{1,0:T(8,128)(2,1)S(1)} %get-tuple-element.513.block_ref), custom_call_target="tpu_custom_call" | custom-call | tf_op jit(solution)/shard_map/cond/branch_27_fun/move_27/pallas_call | solution.py:152
  83.0 0.0 copy-start.1
  83.0 0.0 copy-start.3
  83.0 0.0 copy-start.5
  83.0 30.8 %conditional.4 = ((bf16[8,352,512]{2,1,0:T(8,128)(2,1)}, bf16[544,1024]{1,0:T(8,128)(2,1)})) conditional(s32[]{:T(128)} %bitcast.8, (bf16[352,512]{1,0:T(8,128)(2,1)S(1)}, bf16[544,1024]{1,0:T(8,128)(2,1)S(1)}) %tuple.302, (bf16[352,512]{1,0:T(8,128)(2,1)S(1)}, bf16[544,1024]{1,0:T(8,128)(2,1)S(1)}) %tuple.302, ...), branch_computations={%region_0.0_spmd, %region_1.0_spmd, %region_2.0_spmd, %region_3.0_... | conditional | bytes 8 | solution.py:167
  83.0 30.4 %move_0.3 = (bf16[8,352,512]{2,1,0:T(8,128)(2,1)}, bf16[544,1024]{1,0:T(8,128)(2,1)}) custom-call(bf16[352,512]{1,0:T(8,128)(2,1)S(1)} %get-tuple-element.394.part_ref, bf16[544,1024]{1,0:T(8,128)(2,1)S(1)} %get-tuple-element.395.block_ref), custom_call_target="tpu_custom_call" | custom-call | tf_op jit(solution)/shard_map/cond/branch_0_fun/move_0/pallas_call | solution.py:152
  113.8 0.0 copy-done.1
  113.8 0.0 copy-done.3
  113.8 0.0 copy-done.5
  113.9 0.0 copy-start.4
  113.9 30.8 %finish.1 = (f32[32,1024]{1,0:T(8,128)S(1)}, f32[32,1]{1,0:T(8,128)S(1)}, f32[32,1]{1,0:T(8,128)S(1)}, f32[1,2]{1,0:T(1,128)S(1)}) custom-call(s32[3]{0:T(128)S(1)} %get-tuple-element.638.depth_ref, f32[32,1024]{1,0:T(8,128)S(1)} %bitcast.20, f32[32,1024]{1,0:T(8,128)S(1)} %bitcast.25, f32[32,1024]{1,0:T(8,128)S(1)} %bitcast.22, ...), custom_call_target="tpu_custom_call" | custom-call | tf_op jit(solution)/shard_map/finish/pallas_call | solution.py:340
  144.7 0.0 copy-done.4
  144.7 0.8 result.1
  (1 shorter events, 0.0 us)
Async XLA Ops:
  4.6 0.9 copy-start
  5.5 1.2 copy-start.2
  83.0 30.9 %copy-start.1 = (f32[1024,32]{0,1:T(8,128)S(1)}, f32[1024,32]{0,1:T(8,128)}, u32[]{:S(2)}) copy-start(f32[1024,32]{0,1:T(8,128)} %param.106) | copy-start | bytes 393220
  83.0 30.9 %copy-start.3 = (f32[1024,32]{0,1:T(8,128)S(1)}, f32[1024,32]{0,1:T(8,128)}, u32[]{:S(2)}) copy-start(f32[1024,32]{0,1:T(8,128)} %param.109) | copy-start | bytes 393220
  83.0 30.9 %copy-start.5 = (f32[1024,32]{0,1:T(8,128)S(1)}, f32[1024,32]{0,1:T(8,128)}, u32[]{:S(2)}) copy-start(f32[1024,32]{0,1:T(8,128)} %param.107) | copy-start | bytes 393220
  113.9 30.8 %copy-start.4 = (f32[1024,32]{0,1:T(8,128)S(1)}, f32[1024,32]{0,1:T(8,128)}, u32[]{:S(2)}) copy-start(f32[1024,32]{0,1:T(8,128)} %param.108) | copy-start | bytes 393220
where the time goes:
time: 146 us
  Pallas kernels  138 us (95%)
  between operations  3.39 us (2%)
  local copies, waits for them, and re-layouts  2.74 us (2%)
    pallas_call x3, Pallas kernels, move(): pl.pallas_call(functools.partial(move_kernel, rest), out_shape=(jax.Shape...  106 us
    pallas_call x1, Pallas kernels, finish(): pl.pallas_call(finish_kernel, out_shape=(jax.ShapeDtypeStruct((PROBES, RO...  30.8 us

commit v1 on v0

--- a/solution.py
+++ b/solution.py
@@ -25,7 +25,8 @@
 TALL = DIM + PROBES
 PART = 352
 STARTS = (0, 336, 672)
-PIECE = PART // 2
+HALF = PART // 2
+PIECES = ((0, 96), (96, 80))
 CUTS = (0, 256, 640, 1024)
 SCALE = -GAMMA * math.log2(math.e)
 LOSS = 1e-2
@@ -59,57 +60,42 @@
 
 
 def move_kernel(
-    rest, part_ref, block_ref, ring_ref, b_ref,
-    own_sem, b_send, b_recv, right_send, right_recv, left_send, left_recv,
+    rest, part_ref, block_ref, ring_ref, b_ref, own_sem, b_send, b_recv, ring_send, ring_recv
 ):
     blk, grp = lax.axis_index("blk"), lax.axis_index("grp")
-    z = lax.rem(lax.div(blk, 2), DEEP)
+    z = (blk >> 1) & (DEEP - 1)
     base = blk - 2 * z
-    right = (base + 2 * lax.rem(z + 1, DEEP), grp)
-    left = (base + 2 * lax.rem(z + DEEP - 1, DEEP), grp)
     other = (blk ^ ((rest >> 4) << 4 | (rest >> 3) & 1), grp ^ (rest & 7))
+
+    def along(way):
+        return (base + 2 * ((z + way) & (DEEP - 1)), grp)
+
     barrier = pltpu.get_barrier_semaphore()
-    greeted = [right, left] + ([other] if rest else [])
-    for device in greeted:
+
+    def greet(index, carry):
+        device = along(1 + index * (DEEP - 2))
         pl.semaphore_signal(barrier, inc=1, device_id=device, device_id_type=MESH)
+        return carry
+
+    lax.fori_loop(0, 2, greet, 0)
+    if rest:
+        pl.semaphore_signal(barrier, inc=1, device_id=other, device_id_type=MESH)
     own = pltpu.make_async_copy(part_ref, ring_ref.at[0], own_sem)
     own.start()
-    pl.semaphore_wait(barrier, len(greeted))
-
-    def hop(to, step, piece, send, recvs, sign):
-        rows = pl.ds(piece * PIECE, PIECE)
-        source = lax.rem(DEEP + sign * (step - 1), DEEP)
-        target = lax.rem(DEEP + sign * step, DEEP)
+    pl.semaphore_wait(barrier, 3 if rest else 2)
+
+    def hop(index, step, half, piece):
+        way = 1 + index * (DEEP - 2)
+        rows = pl.ds(half * HALF + PIECES[piece][0], PIECES[piece][1])
         return pltpu.make_async_remote_copy(
-            src_ref=ring_ref.at[source, rows],
-            dst_ref=ring_ref.at[target, rows],
-            send_sem=send,
-            recv_sem=recvs.at[step - 1, piece],
-            device_id=to,
+            src_ref=ring_ref.at[(way * (step - 1)) & (DEEP - 1), rows],
+            dst_ref=ring_ref.at[(way * step) & (DEEP - 1), rows],
+            send_sem=ring_send.at[index, step >> 2],
+            recv_sem=ring_recv.at[index, 4 * (step - 1) + 2 * half + piece],
+            device_id=along(way),
             device_id_type=MESH,
         )
 
-    def rightward(step, piece, send=right_send.at[0]):
-        return hop(right, step, piece, send, right_recv, 1)
-
-    def leftward(step, piece, send=left_send.at[0]):
-        return hop(left, step, piece, send, left_recv, -1)
-
-    def begin(piece, carry):
-        rightward(1, piece).start()
-        leftward(1, piece).start()
-        return carry
-
-    def pass_on(index, carry):
-        step, piece = lax.div(index, 2), lax.rem(index, 2)
-        rightward(step - 1, piece).wait_recv()
-        rightward(step, piece).start()
-        leftward(step - 1, piece).wait_recv()
-        leftward(step, piece).start()
-        return carry
-
-    own.wait()
-    lax.fori_loop(0, 2, begin, 0)
     if rest:
         direct = pltpu.make_async_remote_copy(
             src_ref=block_ref,
@@ -122,33 +108,43 @@
     else:
         direct = pltpu.make_async_copy(block_ref, b_ref, b_send)
     direct.start()
-    lax.fori_loop(4, 8, pass_on, 0)
-    rightward(3, 0).wait_recv()
-    last_right = rightward(4, 0, right_send.at[1])
-    last_right.start()
-    leftward(3, 1).wait_recv()
-    last_left = leftward(4, 1, left_send.at[1])
-    last_left.start()
-    rightward(3, 1).wait_recv()
-    leftward(3, 0).wait_recv()
-    for send in (right_send, left_send):
-        whole = ring_ref.at[pl.ds(0, 3)]
-        pltpu.make_async_remote_copy(
-            src_ref=whole,
-            dst_ref=whole,
-            send_sem=send.at[0],
-            recv_sem=right_recv.at[0, 0],
-            device_id=right,
-            device_id_type=MESH,
-        ).wait_send()
-    last_right.wait()
-    last_left.wait()
+    own.wait()
+
+    def pass_on(count, carry):
+        step, index = count >> 2, count & 1
+        half = ((count >> 1) & 1) + index * (step >> 2)
+        for piece in range(len(PIECES)):
+
+            @pl.when(step > 1)
+            def _():
+                hop(index, step - 1, half, piece).wait_recv()
+
+            hop(index, step, half, piece).start()
+        return carry
+
+    lax.fori_loop(4, 18, pass_on, 0)
+
+    def drain(index, carry):
+        for piece in range(len(PIECES)):
+            hop(index, 3, 1 - index, piece).wait_recv()
+            hop(index, 4, index, piece).wait_recv()
+        for which, whole in enumerate((ring_ref.at[pl.ds(0, 3)], ring_ref.at[0, pl.ds(0, HALF)])):
+            pltpu.make_async_remote_copy(
+                src_ref=whole,
+                dst_ref=whole,
+                send_sem=ring_send.at[index, which],
+                recv_sem=ring_recv.at[0, 0],
+                device_id=along(1),
+                device_id_type=MESH,
+            ).wait_send()
+        return carry
+
+    lax.fori_loop(0, 2, drain, 0)
     direct.wait()
 
 
 def move(rest, part, block):
     one = pltpu.SemaphoreType.DMA
-    sends, recvs = one((2,)), one((4, 2))
     return pl.pallas_call(
         functools.partial(move_kernel, rest),
         out_shape=(
@@ -157,7 +153,7 @@
         ),
         in_specs=[ANY] * 2,
         out_specs=(ANY, ANY),
-        scratch_shapes=[one, one, one, sends, recvs, sends, recvs],
+        scratch_shapes=[one, one, one, one((2, 2)), one((2, 16))],
         compiler_params=params(2 + rest),
         name=f"move_{rest}",
     )(part, block)
@@ -224,7 +220,8 @@
         pl.semaphore_signal(barrier, inc=1, device_id=far_place(k), device_id_type=MESH)
         return carry
 
-    lax.fori_loop(1, 16, greet, 0)
+    for k in range(1, 16):
+        greet(k, 0)
 
     def load_block(s):
         return pltpu.make_async_copy((b0_ref, b1_ref, b2_ref)[s], blocks.at[s], block_sem.at[s])
@@ -237,12 +234,12 @@
     load_part(0).start()
     for s in range(1, ROUNDS):
         load_block(s).start()
-    for part in range(1, ROUNDS):
-        load_part(part).start()
     depths = [depth_ref[s] for s in range(ROUNDS)]
     pieces = []
     for part, gathered in enumerate((g0, g1, g2)):
         load_part(part).wait()
+        if part + 1 < ROUNDS:
+            load_part(part + 1).start()
 
         def one_term(s, carry, part=part, gathered=gathered):
             if part == 0:

time: 146 us -> 144 us (0.986)
  Pallas kernels: 138 us -> 136 us
    pallas_call x3, Pallas kernels: 106 us -> 99.8 us  [move(): pl.pallas_call(functools.partial(move_kernel, rest), out_shape=(jax.Shape...]
    pallas_call x1, Pallas kernels: 30.8 us -> 34.9 us  [finish(): pl.pallas_call(finish_kernel, out_shape=(jax.ShapeDtypeStruct((PROBES, RO...]
where the time goes in v1:
time: 144 us
  Pallas kernels  136 us (94%)
  between operations  3.39 us (2%)
  local copies, waits for them, and re-layouts  2.74 us (2%)
    pallas_call x3, Pallas kernels, move(): pl.pallas_call(functools.partial(move_kernel, rest), out_shape=(jax.Shape...  99.8 us
    pallas_call x1, Pallas kernels, finish(): pl.pallas_call(finish_kernel, out_shape=(jax.ShapeDtypeStruct((PROBES, RO...  34.9 us

profile of v1, /device:TPU:1, one launch (start us, length us, event | category | flops | bytes accessed | tf_op | source)
XLA Modules:
  0.0 144.1 jit_solution(13450971184288923679)
XLA Ops:
  1.3 0.8 and_or_fusion
  2.0 0.6 fusion
  4.6 0.0 copy-start
  4.6 0.9 copy-done
  5.5 0.0 copy-start.2
  5.5 1.2 copy-done.2
  6.7 0.4 prepare.1
  7.1 38.0 %conditional.6 = ((bf16[8,352,512]{2,1,0:T(8,128)(2,1)}, bf16[544,1024]{1,0:T(8,128)(2,1)S(1)})) conditional(s32[]{:T(128)} %bitcast.10, (bf16[352,512]{1,0:T(8,128)(2,1)S(1)}, bf16[544,1024]{1,0:T(8,128)(2,1)S(1)}) %tuple.304, (bf16[352,512]{1,0:T(8,128)(2,1)S(1)}, bf16[544,1024]{1,0:T(8,128)(2,1)S(1)}) %tuple.304, ...), branch_computations={%region_64.0_spmd, %region_65.0_spmd, %region_66.0_spmd, %region_6... | conditional | bytes 8 | solution.py:163
  7.1 37.9 %move_19.5 = (bf16[8,352,512]{2,1,0:T(8,128)(2,1)}, bf16[544,1024]{1,0:T(8,128)(2,1)S(1)}) custom-call(bf16[352,512]{1,0:T(8,128)(2,1)S(1)} %get-tuple-element.560.part_ref, bf16[544,1024]{1,0:T(8,128)(2,1)S(1)} %get-tuple-element.561.block_ref), custom_call_target="tpu_custom_call" | custom-call | tf_op jit(solution)/shard_map/cond/branch_19_fun/move_19/pallas_call | solution.py:148
  45.1 30.6 %conditional.5 = ((bf16[8,352,512]{2,1,0:T(8,128)(2,1)}, bf16[544,1024]{1,0:T(8,128)(2,1)})) conditional(s32[]{:T(128)} %bitcast.9, (bf16[352,512]{1,0:T(8,128)(2,1)S(1)}, bf16[544,1024]{1,0:T(8,128)(2,1)S(1)}) %tuple.303, (bf16[352,512]{1,0:T(8,128)(2,1)S(1)}, bf16[544,1024]{1,0:T(8,128)(2,1)S(1)}) %tuple.303, ...), branch_computations={%region_32.0_spmd, %region_33.0_spmd, %region_34.0_spmd, %region_3... | conditional | bytes 8 | solution.py:163
  45.3 30.1 %move_10.4 = (bf16[8,352,512]{2,1,0:T(8,128)(2,1)}, bf16[544,1024]{1,0:T(8,128)(2,1)}) custom-call(bf16[352,512]{1,0:T(8,128)(2,1)S(1)} %get-tuple-element.478.part_ref, bf16[544,1024]{1,0:T(8,128)(2,1)S(1)} %get-tuple-element.479.block_ref), custom_call_target="tpu_custom_call" | custom-call | tf_op jit(solution)/shard_map/cond/branch_10_fun/move_10/pallas_call | solution.py:148
  75.7 0.0 copy-start.1
  75.7 0.0 copy-start.3
  75.7 0.0 copy-start.5
  75.7 32.4 %conditional.4 = ((bf16[8,352,512]{2,1,0:T(8,128)(2,1)}, bf16[544,1024]{1,0:T(8,128)(2,1)})) conditional(s32[]{:T(128)} %bitcast.8, (bf16[352,512]{1,0:T(8,128)(2,1)S(1)}, bf16[544,1024]{1,0:T(8,128)(2,1)S(1)}) %tuple.302, (bf16[352,512]{1,0:T(8,128)(2,1)S(1)}, bf16[544,1024]{1,0:T(8,128)(2,1)S(1)}) %tuple.302, ...), branch_computations={%region_0.0_spmd, %region_1.0_spmd, %region_2.0_spmd, %region_3.0_... | conditional | bytes 8 | solution.py:163
  75.8 31.8 %move_18.3 = (bf16[8,352,512]{2,1,0:T(8,128)(2,1)}, bf16[544,1024]{1,0:T(8,128)(2,1)}) custom-call(bf16[352,512]{1,0:T(8,128)(2,1)S(1)} %get-tuple-element.430.part_ref, bf16[544,1024]{1,0:T(8,128)(2,1)S(1)} %get-tuple-element.431.block_ref), custom_call_target="tpu_custom_call" | custom-call | tf_op jit(solution)/shard_map/cond/branch_18_fun/move_18/pallas_call | solution.py:148
  108.2 0.0 copy-done.1
  108.2 0.0 copy-done.3
  108.2 0.0 copy-done.5
  108.2 0.0 copy-start.4
  108.2 34.9 %finish.1 = (f32[32,1024]{1,0:T(8,128)S(1)}, f32[32,1]{1,0:T(8,128)S(1)}, f32[32,1]{1,0:T(8,128)S(1)}, f32[1,2]{1,0:T(1,128)S(1)}) custom-call(s32[3]{0:T(128)S(1)} %get-tuple-element.638.depth_ref, f32[32,1024]{1,0:T(8,128)S(1)} %bitcast.20, f32[32,1024]{1,0:T(8,128)S(1)} %bitcast.25, f32[32,1024]{1,0:T(8,128)S(1)} %bitcast.22, ...), custom_call_target="tpu_custom_call" | custom-call | tf_op jit(solution)/shard_map/finish/pallas_call | solution.py:337
  143.2 0.0 copy-done.4
  143.2 0.8 result.1
  (1 shorter events, 0.0 us)
Async XLA Ops:
  4.6 0.9 copy-start
  5.5 1.2 copy-start.2
  75.7 32.5 %copy-start.1 = (f32[1024,32]{0,1:T(8,128)S(1)}, f32[1024,32]{0,1:T(8,128)}, u32[]{:S(2)}) copy-start(f32[1024,32]{0,1:T(8,128)} %param.106) | copy-start | bytes 393220
  75.7 32.5 %copy-start.3 = (f32[1024,32]{0,1:T(8,128)S(1)}, f32[1024,32]{0,1:T(8,128)}, u32[]{:S(2)}) copy-start(f32[1024,32]{0,1:T(8,128)} %param.109) | copy-start | bytes 393220
  75.7 32.5 %copy-start.5 = (f32[1024,32]{0,1:T(8,128)S(1)}, f32[1024,32]{0,1:T(8,128)}, u32[]{:S(2)}) copy-start(f32[1024,32]{0,1:T(8,128)} %param.107) | copy-start | bytes 393220
  108.2 35.0 %copy-start.4 = (f32[1024,32]{0,1:T(8,128)S(1)}, f32[1024,32]{0,1:T(8,128)}, u32[]{:S(2)}) copy-start(f32[1024,32]{0,1:T(8,128)} %param.108) | copy-start | bytes 393220

commit v2 on v1

--- a/solution.py
+++ b/solution.py
@@ -30,6 +30,7 @@
 CUTS = (0, 256, 640, 1024)
 SCALE = -GAMMA * math.log2(math.e)
 LOSS = 1e-2
+TINY = 1e-25
 
 
 def params(collective_id=None):
@@ -263,7 +264,8 @@
         if part == 0:
             pl.semaphore_wait(barrier, 30)
 
-        def give_back(k, carry, part=part, columns=columns, lanes=lanes):
+        def give_back(count, carry, part=part, columns=columns, lanes=lanes):
+            k = lax.rem(count + 2, DEEP - 1) + 1
             meant = sum(
                 jnp.where(depths[s] == k, terms[s, :, columns], 0.0) for s in range(ROUNDS)
             )
@@ -302,26 +304,20 @@
         image_ref[:, cut] = image
         for q, (a, b) in enumerate(((r, r), (d, image), (r, image), (image, image))):
             columns[q] = columns[q] + jnp.sum(a * b, axis=1, keepdims=True)
-    lane = lax.broadcasted_iota(jnp.int32, (8, 128), 1)
-    packed = jnp.zeros((8, 128), F32)
-    for q, column in enumerate(columns):
-        for g in range(4):
-            packed = jnp.where(lane == q * 4 + g, column[g * 8 : g * 8 + 8], packed)
-    near[0] = packed
+    near[0] = jnp.broadcast_to(jnp.concatenate(columns, axis=0), (128, 128)).T[:1]
     first = exchange(near, near_send, near_recv, near_place)
     far[0] = tree(near)
     second = exchange(far, far_send, far_recv, far_place)
     total = tree(far)
-    norm, curv, cross, square = (
-        jnp.concatenate([total[:, q * 4 + g : q * 4 + g + 1] for g in range(4)], axis=0)
-        for q in range(4)
-    )
+    column = jnp.broadcast_to(total, (128, 128)).T[:, :1]
+    norm, curv, cross, square = (column[q * PROBES : (q + 1) * PROBES] for q in range(4))
     alpha = norm / curv
     alpha_ref[...] = alpha
-    twice, quad = 2.0 * alpha * cross, alpha * alpha * square
+    twice, quad = 2.0 * alpha * cross, alpha * (alpha * square)
     following = norm - twice + quad
     good = following >= LOSS * (norm + jnp.abs(twice) + quad)
     good = jnp.logical_and(good, following < 3e38)
+    good = jnp.logical_and(good, jnp.minimum(norm, square) > TINY)
     beta_ref[...] = following / norm
     bad_ref[0, 0] = jnp.max(jnp.where(good, 0.0, 1.0))
     bad_ref[0, 1] = 0.0
@@ -348,7 +344,7 @@
         + [pltpu.VMEM((ROUNDS, TALL, ROWS), BF16), pltpu.VMEM((ROUNDS, 1, ROWS), F32)]
         + [pltpu.VMEM((ROUNDS, PROBES, ROWS), F32)]
         + [pltpu.VMEM((DEEP, PROBES, ROWS), BF16)] * 2
-        + [pltpu.VMEM((16, 8, 128), F32)] * 2
+        + [pltpu.VMEM((16, 1, 128), F32)] * 2
         + [dma((3,))] * 4 + [dma] * 4,
         compiler_params=params(1),
         name="finish",

time: 144 us -> 142 us (0.986)
  Pallas kernels: 136 us -> 134 us
    pallas_call x1, Pallas kernels: 34.9 us -> 30.1 us  [finish(): pl.pallas_call(finish_kernel, out_shape=(jax.ShapeDtypeStruct((PROBES, RO...]
    pallas_call x3, Pallas kernels: 99.8 us -> 103 us  [move(): pl.pallas_call(functools.partial(move_kernel, rest), out_shape=(jax.Shape...]
where the time goes in v2:
time: 142 us
  Pallas kernels  134 us (94%)
  between operations  3.39 us (2%)
  local copies, waits for them, and re-layouts  2.74 us (2%)
    pallas_call x3, Pallas kernels, move(): pl.pallas_call(functools.partial(move_kernel, rest), out_shape=(jax.Shape...  103 us
    pallas_call x1, Pallas kernels, finish(): pl.pallas_call(finish_kernel, out_shape=(jax.ShapeDtypeStruct((PROBES, RO...  30.1 us

profile of v2, /device:TPU:1, one launch (start us, length us, event | category | flops | bytes accessed | tf_op | source)
XLA Modules:
  0.0 141.9 jit_solution(8273456194051477067)
XLA Ops:
  1.3 0.8 and_or_fusion
  2.0 0.6 fusion
  4.6 0.0 copy-start
  4.6 0.9 copy-done
  5.5 0.0 copy-start.2
  5.5 1.2 copy-done.2
  6.7 0.4 prepare.1
  7.1 37.0 %conditional.6 = ((bf16[8,352,512]{2,1,0:T(8,128)(2,1)}, bf16[544,1024]{1,0:T(8,128)(2,1)S(1)})) conditional(s32[]{:T(128)} %bitcast.10, (bf16[352,512]{1,0:T(8,128)(2,1)S(1)}, bf16[544,1024]{1,0:T(8,128)(2,1)S(1)}) %tuple.304, (bf16[352,512]{1,0:T(8,128)(2,1)S(1)}, bf16[544,1024]{1,0:T(8,128)(2,1)S(1)}) %tuple.304, ...), branch_computations={%region_64.0_spmd, %region_65.0_spmd, %region_66.0_spmd, %region_6... | conditional | bytes 8 | solution.py:164
  7.1 36.9 %move_17.5 = (bf16[8,352,512]{2,1,0:T(8,128)(2,1)}, bf16[544,1024]{1,0:T(8,128)(2,1)S(1)}) custom-call(bf16[352,512]{1,0:T(8,128)(2,1)S(1)} %get-tuple-element.556.part_ref, bf16[544,1024]{1,0:T(8,128)(2,1)S(1)} %get-tuple-element.557.block_ref), custom_call_target="tpu_custom_call" | custom-call | tf_op jit(solution)/shard_map/cond/branch_17_fun/move_17/pallas_call | solution.py:149
  44.0 31.1 %conditional.5 = ((bf16[8,352,512]{2,1,0:T(8,128)(2,1)}, bf16[544,1024]{1,0:T(8,128)(2,1)})) conditional(s32[]{:T(128)} %bitcast.9, (bf16[352,512]{1,0:T(8,128)(2,1)S(1)}, bf16[544,1024]{1,0:T(8,128)(2,1)S(1)}) %tuple.303, (bf16[352,512]{1,0:T(8,128)(2,1)S(1)}, bf16[544,1024]{1,0:T(8,128)(2,1)S(1)}) %tuple.303, ...), branch_computations={%region_32.0_spmd, %region_33.0_spmd, %region_34.0_spmd, %region_3... | conditional | bytes 8 | solution.py:164
  44.3 30.8 %move_19.4 = (bf16[8,352,512]{2,1,0:T(8,128)(2,1)}, bf16[544,1024]{1,0:T(8,128)(2,1)}) custom-call(bf16[352,512]{1,0:T(8,128)(2,1)S(1)} %get-tuple-element.496.part_ref, bf16[544,1024]{1,0:T(8,128)(2,1)S(1)} %get-tuple-element.497.block_ref), custom_call_target="tpu_custom_call" | custom-call | tf_op jit(solution)/shard_map/cond/branch_19_fun/move_19/pallas_call | solution.py:149
  75.1 0.0 copy-start.1
  75.1 0.0 copy-start.3
  75.1 0.0 copy-start.5
  75.1 35.7 %conditional.4 = ((bf16[8,352,512]{2,1,0:T(8,128)(2,1)}, bf16[544,1024]{1,0:T(8,128)(2,1)})) conditional(s32[]{:T(128)} %bitcast.8, (bf16[352,512]{1,0:T(8,128)(2,1)S(1)}, bf16[544,1024]{1,0:T(8,128)(2,1)S(1)}) %tuple.302, (bf16[352,512]{1,0:T(8,128)(2,1)S(1)}, bf16[544,1024]{1,0:T(8,128)(2,1)S(1)}) %tuple.302, ...), branch_computations={%region_0.0_spmd, %region_1.0_spmd, %region_2.0_spmd, %region_3.0_... | conditional | bytes 8 | solution.py:164
  75.5 35.1 %move_29.3 = (bf16[8,352,512]{2,1,0:T(8,128)(2,1)}, bf16[544,1024]{1,0:T(8,128)(2,1)}) custom-call(bf16[352,512]{1,0:T(8,128)(2,1)S(1)} %get-tuple-element.452.part_ref, bf16[544,1024]{1,0:T(8,128)(2,1)S(1)} %get-tuple-element.453.block_ref), custom_call_target="tpu_custom_call" | custom-call | tf_op jit(solution)/shard_map/cond/branch_29_fun/move_29/pallas_call | solution.py:149
  110.9 0.0 copy-done.1
  110.9 0.0 copy-done.3
  110.9 0.0 copy-done.5
  110.9 0.0 copy-start.4
  110.9 30.1 %finish.1 = (f32[32,1024]{1,0:T(8,128)S(1)}, f32[32,1]{1,0:T(8,128)S(1)}, f32[32,1]{1,0:T(8,128)S(1)}, f32[1,2]{1,0:T(1,128)S(1)}) custom-call(s32[3]{0:T(128)S(1)} %get-tuple-element.638.depth_ref, f32[32,1024]{1,0:T(8,128)S(1)} %bitcast.20, f32[32,1024]{1,0:T(8,128)S(1)} %bitcast.25, f32[32,1024]{1,0:T(8,128)S(1)} %bitcast.22, ...), custom_call_target="tpu_custom_call" | custom-call | tf_op jit(solution)/shard_map/finish/pallas_call | solution.py:333
  141.1 0.0 copy-done.4
  141.1 0.8 result.1
  (1 shorter events, 0.0 us)
Async XLA Ops:
  4.6 0.9 copy-start
  5.5 1.2 copy-start.2
  75.1 35.8 %copy-start.1 = (f32[1024,32]{0,1:T(8,128)S(1)}, f32[1024,32]{0,1:T(8,128)}, u32[]{:S(2)}) copy-start(f32[1024,32]{0,1:T(8,128)} %param.106) | copy-start | bytes 393220
  75.1 35.8 %copy-start.3 = (f32[1024,32]{0,1:T(8,128)S(1)}, f32[1024,32]{0,1:T(8,128)}, u32[]{:S(2)}) copy-start(f32[1024,32]{0,1:T(8,128)} %param.109) | copy-start | bytes 393220
  75.1 35.8 %copy-start.5 = (f32[1024,32]{0,1:T(8,128)S(1)}, f32[1024,32]{0,1:T(8,128)}, u32[]{:S(2)}) copy-start(f32[1024,32]{0,1:T(8,128)} %param.107) | copy-start | bytes 393220
  110.9 30.2 %copy-start.4 = (f32[1024,32]{0,1:T(8,128)S(1)}, f32[1024,32]{0,1:T(8,128)}, u32[]{:S(2)}) copy-start(f32[1024,32]{0,1:T(8,128)} %param.108) | copy-start | bytes 393220

commit v3 on v2

--- a/solution.py
+++ b/solution.py
@@ -27,7 +27,7 @@
 STARTS = (0, 336, 672)
 HALF = PART // 2
 PIECES = ((0, 96), (96, 80))
-CUTS = (0, 256, 640, 1024)
+CUTS = (0, 256, 512, 1024)
 SCALE = -GAMMA * math.log2(math.e)
 LOSS = 1e-2
 TINY = 1e-25
@@ -41,11 +41,17 @@
     )
 
 
-def prepare_kernel(x_ref, d_ref, out_ref, p0_ref, p1_ref, p2_ref):
-    out_ref[:DIM] = x_ref[...].T
-    out_ref[DIM:] = d_ref[...].astype(BF16)
+def prepare_kernel(x_ref, d_ref, out_ref, p0_ref, p1_ref, p2_ref, x, d, sems):
+    load_x = pltpu.make_async_copy(x_ref, x, sems.at[0])
+    load_d = pltpu.make_async_copy(d_ref, d, sems.at[1])
+    load_x.start()
+    load_d.start()
+    load_x.wait()
+    out_ref[:DIM] = x[...].T
     for ref, start in zip((p0_ref, p1_ref, p2_ref), STARTS):
-        ref[...] = x_ref[start : start + PART]
+        ref[...] = x[start : start + PART]
+    load_d.wait()
+    out_ref[DIM:] = d[...].astype(BF16)
 
 
 def prepare(embedding, dir_t):
@@ -53,9 +59,14 @@
     return pl.pallas_call(
         prepare_kernel,
         out_shape=(jax.ShapeDtypeStruct((TALL, ROWS), BF16), part, part, part),
-        in_specs=[VMEM] * 2,
+        in_specs=[ANY] * 2,
         out_specs=(VMEM,) * 4,
-        compiler_params=params(),
+        scratch_shapes=[
+            pltpu.VMEM((ROWS, DIM), BF16),
+            pltpu.VMEM((PROBES, ROWS), F32),
+            pltpu.SemaphoreType.DMA((2,)),
+        ],
+        compiler_params=pltpu.CompilerParams(vmem_limit_bytes=60 * 2**20),
         name="prepare",
     )(embedding, dir_t)
 

time: 142 us -> 141 us (level)
  local copies, waits for them, and re-layouts: 2.74 us -> 0.62 us
    pallas_call x3, Pallas kernels: 103 us -> 98.6 us  [move(): pl.pallas_call(functools.partial(move_kernel, rest), out_shape=(jax.Shape...]
    pallas_call x1, Pallas kernels: 30.1 us -> 33.8 us  [finish(): pl.pallas_call(finish_kernel, out_shape=(jax.ShapeDtypeStruct((PROBES, RO...]
    unnamed x12 -> x8, local copies, waits for them, and re-layouts: 2.15 us -> 0.03 us
where the time goes in v3:
time: 141 us
  Pallas kernels  135 us (96%)
  between operations  3.38 us (2%)
    pallas_call x3, Pallas kernels, move(): pl.pallas_call(functools.partial(move_kernel, rest), out_shape=(jax.Shape...  98.6 us
    pallas_call x1, Pallas kernels, finish(): pl.pallas_call(finish_kernel, out_shape=(jax.ShapeDtypeStruct((PROBES, RO...  33.8 us

profile of v3, /device:TPU:1, one launch (start us, length us, event | category | flops | bytes accessed | tf_op | source)
XLA Modules:
  0.0 140.6 jit_solution(2873091038246846516)
XLA Ops:
  1.3 0.8 and_or_fusion
  2.0 0.6 fusion
  4.6 1.7 %prepare.1 = (bf16[544,1024]{1,0:T(8,128)(2,1)S(1)}, bf16[352,512]{1,0:T(8,128)(2,1)S(1)}, bf16[352,512]{1,0:T(8,128)(2,1)S(1)}, bf16[352,512]{1,0:T(8,128)(2,1)S(1)}) custom-call(bf16[1024,512]{1,0:T(8,128)(2,1)} %x_ref.1, f32[32,1024]{1,0:T(8,128)} %bitcast.19), custom_call_target="tpu_custom_call" | custom-call | tf_op jit(solution)/shard_map/prepare/pallas_call | solution.py:59
  6.3 38.3 %conditional.6 = ((bf16[8,352,512]{2,1,0:T(8,128)(2,1)}, bf16[544,1024]{1,0:T(8,128)(2,1)S(1)})) conditional(s32[]{:T(128)} %bitcast.10, (bf16[352,512]{1,0:T(8,128)(2,1)S(1)}, bf16[544,1024]{1,0:T(8,128)(2,1)S(1)}) %tuple.304, (bf16[352,512]{1,0:T(8,128)(2,1)S(1)}, bf16[544,1024]{1,0:T(8,128)(2,1)S(1)}) %tuple.304, ...), branch_computations={%region_64.0_spmd, %region_65.0_spmd, %region_66.0_spmd, %region_6... | conditional | bytes 8 | solution.py:175
  6.3 38.2 %move_5.5 = (bf16[8,352,512]{2,1,0:T(8,128)(2,1)}, bf16[544,1024]{1,0:T(8,128)(2,1)S(1)}) custom-call(bf16[352,512]{1,0:T(8,128)(2,1)S(1)} %get-tuple-element.532.part_ref, bf16[544,1024]{1,0:T(8,128)(2,1)S(1)} %get-tuple-element.533.block_ref), custom_call_target="tpu_custom_call" | custom-call | tf_op jit(solution)/shard_map/cond/branch_5_fun/move_5/pallas_call | solution.py:160
  44.6 31.4 %conditional.5 = ((bf16[8,352,512]{2,1,0:T(8,128)(2,1)}, bf16[544,1024]{1,0:T(8,128)(2,1)})) conditional(s32[]{:T(128)} %bitcast.9, (bf16[352,512]{1,0:T(8,128)(2,1)S(1)}, bf16[544,1024]{1,0:T(8,128)(2,1)S(1)}) %tuple.303, (bf16[352,512]{1,0:T(8,128)(2,1)S(1)}, bf16[544,1024]{1,0:T(8,128)(2,1)S(1)}) %tuple.303, ...), branch_computations={%region_32.0_spmd, %region_33.0_spmd, %region_34.0_spmd, %region_3... | conditional | bytes 8 | solution.py:175
  44.8 30.9 %move_10.4 = (bf16[8,352,512]{2,1,0:T(8,128)(2,1)}, bf16[544,1024]{1,0:T(8,128)(2,1)}) custom-call(bf16[352,512]{1,0:T(8,128)(2,1)S(1)} %get-tuple-element.478.part_ref, bf16[544,1024]{1,0:T(8,128)(2,1)S(1)} %get-tuple-element.479.block_ref), custom_call_target="tpu_custom_call" | custom-call | tf_op jit(solution)/shard_map/cond/branch_10_fun/move_10/pallas_call | solution.py:160
  76.0 0.0 copy-start
  76.0 0.0 copy-start.1
  76.0 0.0 copy-start.3
  76.0 29.8 %conditional.4 = ((bf16[8,352,512]{2,1,0:T(8,128)(2,1)}, bf16[544,1024]{1,0:T(8,128)(2,1)})) conditional(s32[]{:T(128)} %bitcast.8, (bf16[352,512]{1,0:T(8,128)(2,1)S(1)}, bf16[544,1024]{1,0:T(8,128)(2,1)S(1)}) %tuple.302, (bf16[352,512]{1,0:T(8,128)(2,1)S(1)}, bf16[544,1024]{1,0:T(8,128)(2,1)S(1)}) %tuple.302, ...), branch_computations={%region_0.0_spmd, %region_1.0_spmd, %region_2.0_spmd, %region_3.0_... | conditional | bytes 8 | solution.py:175
  76.1 29.4 %move_1.3 = (bf16[8,352,512]{2,1,0:T(8,128)(2,1)}, bf16[544,1024]{1,0:T(8,128)(2,1)}) custom-call(bf16[352,512]{1,0:T(8,128)(2,1)S(1)} %get-tuple-element.396.part_ref, bf16[544,1024]{1,0:T(8,128)(2,1)S(1)} %get-tuple-element.397.block_ref), custom_call_target="tpu_custom_call" | custom-call | tf_op jit(solution)/shard_map/cond/branch_1_fun/move_1/pallas_call | solution.py:160
  105.9 0.0 copy-done
  105.9 0.0 copy-done.1
  105.9 0.0 copy-done.3
  105.9 0.0 copy-start.2
  105.9 33.8 %finish.1 = (f32[32,1024]{1,0:T(8,128)S(1)}, f32[32,1]{1,0:T(8,128)S(1)}, f32[32,1]{1,0:T(8,128)S(1)}, f32[1,2]{1,0:T(1,128)S(1)}) custom-call(s32[3]{0:T(128)S(1)} %get-tuple-element.638.depth_ref, f32[32,1024]{1,0:T(8,128)S(1)} %bitcast.20, f32[32,1024]{1,0:T(8,128)S(1)} %bitcast.25, f32[32,1024]{1,0:T(8,128)S(1)} %bitcast.22, ...), custom_call_target="tpu_custom_call" | custom-call | tf_op jit(solution)/shard_map/finish/pallas_call | solution.py:344
  139.7 0.0 copy-done.2
  139.7 0.8 result.1
  (1 shorter events, 0.0 us)
Async XLA Ops:
  76.0 29.9 %copy-start = (f32[1024,32]{0,1:T(8,128)S(1)}, f32[1024,32]{0,1:T(8,128)}, u32[]{:S(2)}) copy-start(f32[1024,32]{0,1:T(8,128)} %param.106) | copy-start | bytes 393220
  76.0 29.9 %copy-start.1 = (f32[1024,32]{0,1:T(8,128)S(1)}, f32[1024,32]{0,1:T(8,128)}, u32[]{:S(2)}) copy-start(f32[1024,32]{0,1:T(8,128)} %param.109) | copy-start | bytes 393220
  76.0 29.9 %copy-start.3 = (f32[1024,32]{0,1:T(8,128)S(1)}, f32[1024,32]{0,1:T(8,128)}, u32[]{:S(2)}) copy-start(f32[1024,32]{0,1:T(8,128)} %param.107) | copy-start | bytes 393220
  105.9 33.8 %copy-start.2 = (f32[1024,32]{0,1:T(8,128)S(1)}, f32[1024,32]{0,1:T(8,128)}, u32[]{:S(2)}) copy-start(f32[1024,32]{0,1:T(8,128)} %param.108) | copy-start | bytes 393220
